TPU v7x, 128 devices: a whole 4x4x4 slice. The times are simulated.
128 devices in a mesh: gx: 16 (over z_hi, x, core), gy: 8 (over z_lo, y).
Axes of the slice: x: 4, y: 4, z: 4 (z_hi: 2, z_lo: 2; z = z_hi * 2 + z_lo), core: 2. Of those that a mesh axis runs over, the one named last changes fastest.
Arguments:
- state: float32 [64, 8, 256, 1024], P(None, None, 'gx', 'gy'), may hold values from -6 to 6
- east_wind: float32 [64, 256, 1024], P(None, 'gx', 'gy'), may hold values from -0.24 to 0.24
- north_wind: float32 [64, 256, 1024], P(None, 'gx', 'gy'), may hold values from -0.24 to 0.24
- kappa: float32 [63, 256, 1024], P(None, 'gx', 'gy'), may hold values from 0.05 to 500
- w_in: bfloat16 [256, 512], replicated, may hold values from -0.375 to 0.375
- w_mid: bfloat16 [512, 512], replicated, may hold values from -0.25 to 0.25
- w_out: bfloat16 [512, 256], replicated, may hold values from -0.25 to 0.25
- cotangent: bfloat16 [262144, 256], P(('gx', 'gy')), may hold values from -6 to 6
Outputs:
- new_state: float32 [64, 8, 256, 1024], P(None, None, 'gx', 'gy')
- adjoint: bfloat16 [262144, 256], P(('gx', 'gy'))
All inputs are finite; a program needn't handle non-finite values.
Results may differ from a plain program's by a relative error of at most 0.006.
The roundings to bfloat16 on the way count: a program that leaves them out, or rounds other values in their place, can miss the bound.
Values may be sent and summed in bfloat16 or wider, within the bound.
No kernel may reach another device: no remote copies, remote signals or barrier semaphores. Data moves between devices by JAX's collectives and lax.ppermute only.
A program may use at most 128 MiB of HBM per device.

v0:
```python
import functools

import jax
import jax.numpy as jnp
from jax import lax
from jax.experimental import pallas as pl
from jax.experimental.pallas import tpu as pltpu
from jax.sharding import PartitionSpec as P

F32 = jnp.float32
BF16 = jnp.bfloat16
LEVELS, FIELDS, ROWS, COLS = 64, 8, 16, 128
KINDS = 4
HIDDEN, FEATURES = 512, 256
HALF = LEVELS // 2
ROW_MESSAGE = 2 * LEVELS * FIELDS + 3 * LEVELS
COL_MESSAGE = 2 * (FIELDS * ROWS + 2 * ROWS + 3 * FIELDS)
UNROLL = 4


def at_end(axis):
    return lax.axis_index(axis) == lax.axis_size(axis) - 1


def lanes(shape):
    return lax.broadcasted_iota(jnp.int32, shape, len(shape) - 1)


def is_odd(axis):
    return lax.axis_index(axis) % 2 == 1


def rows_kernel(state, east, north, partner, other):
    closed = (lanes((LEVELS, COLS)) == COLS - 1) & at_end("gy")
    count = LEVELS * FIELDS

    def fill(out, near, far):
        for f in range(FIELDS):
            at = f * LEVELS
            out[at : at + LEVELS, :] = state[pl.ds(f * ROWS + near, LEVELS, stride=FIELDS * ROWS), :].astype(BF16)
            at += count
            out[at : at + LEVELS, :] = state[pl.ds(f * ROWS + far, LEVELS, stride=FIELDS * ROWS), :].astype(BF16)
        base = 2 * count
        out[base : base + LEVELS, :] = east[pl.ds(near, LEVELS, stride=ROWS), :].astype(BF16)
        out[base + LEVELS : base + 2 * LEVELS, :] = east[pl.ds(far, LEVELS, stride=ROWS), :].astype(BF16)
        north_near = north[pl.ds(near, LEVELS, stride=ROWS), :]
        out[base + 2 * LEVELS : base + 3 * LEVELS, :] = jnp.where(closed, 0.0, north_near).astype(BF16)

    @pl.when(is_odd("gx"))
    def _():
        fill(partner, 0, 1)
        fill(other, ROWS - 1, ROWS - 2)

    @pl.when(~is_odd("gx"))
    def _():
        fill(partner, ROWS - 1, ROWS - 2)
        fill(other, 0, 1)


def spread_winds(winds, above, below):
    base = 2 * LEVELS * FIELDS
    winds[0 : 3 * LEVELS, :] = above[base : base + 3 * LEVELS, :].astype(winds.dtype)
    winds[3 * LEVELS : 4 * LEVELS, :] = below[base : base + LEVELS, :].astype(winds.dtype)
    winds[4 * LEVELS : 5 * LEVELS, :] = below[base + 2 * LEVELS : base + 3 * LEVELS, :].astype(winds.dtype)
    winds[5 * LEVELS : 8 * LEVELS, :] = jnp.zeros((3 * LEVELS, COLS), winds.dtype)


def ones_where(shape, rule):
    row = lax.broadcasted_iota(jnp.int32, shape, 0)
    col = lax.broadcasted_iota(jnp.int32, shape, 1)
    return jnp.where(rule(row, col), 1.0, 0.0).astype(BF16)


def edge_matrix():
    return ones_where((COLS, COLS), lambda row, col: (row + 2) % COLS == col % 4)


def cols_kernel(state, east, north, w_in, w_mid, w_out, out, *prepared):
    prepare(w_in, w_mid, w_out, *prepared)
    per_level = FIELDS * ROWS
    gather = edge_matrix()
    row = lax.broadcasted_iota(jnp.int32, (ROWS, COLS), 0)
    lane = lanes((ROWS, COLS))
    many = 16
    for b in range(2):

        def body(step, totals):
            level = b * HALF + step * many
            merged = list(totals)
            for n, (ref, size) in enumerate(((state, per_level), (east, ROWS), (north, ROWS))):
                at = pl.ds(pl.multiple_of(level * size, size), many * size)
                edges = dot(ref[at, :].astype(BF16), gather)
                for k in range(many):
                    mine = (lanes((size, COLS)) // 4) == step * many + k
                    merged[n] = jnp.where(mine, edges[k * size : (k + 1) * size], merged[n])
            return tuple(merged)

        start = tuple(jnp.zeros((n, COLS), F32) for n in (per_level, ROWS, ROWS))
        fields, east_edge, north_edge = lax.fori_loop(0, HALF // many, body, start)
        east_edge = jnp.where((row == ROWS - 1) & at_end("gx"), 0.0, east_edge)
        north_edge = jnp.where((lane % 4 == 1) & at_end("gy"), 0.0, north_edge)
        out[b * per_level : (b + 1) * per_level, :] = fields.astype(BF16)
        base = 2 * per_level
        out[base + b * ROWS : base + (b + 1) * ROWS, :] = east_edge.astype(BF16)
        base += 2 * ROWS
        out[base + b * ROWS : base + (b + 1) * ROWS, :] = north_edge.astype(BF16)


def corners_kernel(edges, from_partner, from_other, out, winds):
    @pl.when(is_odd("gx"))
    def _():
        corners(edges, from_partner, from_other, out, winds)

    @pl.when(~is_odd("gx"))
    def _():
        corners(edges, from_other, from_partner, out, winds)


def corners(edges, above, below, out, winds):
    count = LEVELS * FIELDS
    spread_winds(winds, above, below)
    gather = edge_matrix()
    collect = ones_where(
        (16, count), lambda row, col: (row % 8 == col // LEVELS) & (row // 8 == (col % LEVELS) // HALF)
    )
    level = lax.broadcasted_iota(jnp.int32, (count, COLS), 0) % HALF
    mine = lanes((count, COLS)) // 4 == level
    size = edges.shape[0]
    out[0:size, :] = edges[...]
    for n, source in enumerate((above[0:count, :], below[0:count, :], winds[...])):
        spread = jnp.where(mine, dot(source, gather), 0.0).astype(BF16)
        out[size + 16 * n : size + 16 * (n + 1), :] = dot(collect, spread).astype(BF16)


def prepare(w_in, w_mid, w_out, w_in_t, w_mid_t, w_out_t):
    by_level = ones_where(
        (FEATURES, FEATURES), lambda row, col: row == (col % KINDS) * LEVELS + col // KINDS
    )
    w_in_t[...] = dot(w_in[...].T, by_level).astype(BF16)
    w_mid_t[...] = w_mid[...].T
    w_out_t[...] = dot(w_out[...], by_level).astype(BF16).T


def coefficients(east_up, east, north_left, north):
    zero = 0.0
    east_plus, east_minus = jnp.maximum(east_up, zero), jnp.minimum(east, zero)
    north_plus, north_minus = jnp.maximum(north_left, zero), jnp.minimum(north, zero)
    centre = (
        1.0
        - (jnp.maximum(east, zero) - jnp.minimum(east_up, zero))
        - (jnp.maximum(north, zero) - jnp.minimum(north_left, zero))
    )
    return centre, east_plus, -east_minus, north_plus, -north_minus


def combine(coefs, here, up, down, left, right):
    centre, from_up, from_down, from_left, from_right = coefs
    return centre * here + (from_up * up + from_down * down) + (from_left * left + from_right * right)


def beside_matrix():
    def rule(row, col):
        lane, place = row % COLS, col % COLS
        inside = either(col < COLS, lane + 1 == place, lane == place + 1)
        halo = either(col < COLS, (place == 0) & (lane % 4 == 1), (place == COLS - 1) & (lane % 4 == 2))
        return either(row < 2 * COLS, inside, halo)

    return ones_where((3 * COLS, 2 * COLS), rule)


def strip_matrix():
    def rule(row, col):
        lane, place = row % COLS, col % COLS
        theirs = row < COLS
        one, two = place % 4 == 1, place % 4 == 2
        left = (lane + 1 == place) & either(theirs, one, two)
        right = (lane == place + 1) & either(theirs, two, one)
        return either(col < COLS, left, right)

    return ones_where((2 * COLS, 2 * COLS), rule)


def either(choice, yes, no):
    return (choice & yes) | (~choice & no)


def high_low(values):
    high = values.astype(BF16)
    return high, (values - high.astype(F32)).astype(BF16)


BATCH = 32
SLICE = KINDS * ROWS


def advance(begin, refs, each_start, each_batch, scratch):
    state, far_east_wind, far_north, far_kappa, rows_partner, rows_other, own, from_partner, from_other = refs
    (above, below, held, winds, near_up, near_down, pass_up, pass_down, edge_state, edge_pass, edge_north, first_pass,
     moving, moving_north, beside_map, east, north, kappa, ratio, sems) = scratch
    count = LEVELS * FIELDS
    per_level = FIELDS * ROWS
    batches = LEVELS // BATCH
    copies = [
        pltpu.make_async_copy(
            state.at[pl.ds(n * BATCH, BATCH), pl.ds(begin * ROWS, SLICE), :],
            held.at[pl.ds(1 + n * BATCH, BATCH)],
            sems.at[n],
        )
        for n in range(batches)
    ]
    planes = ((far_east_wind, east), (far_north, north), (far_kappa, kappa))
    later = [pltpu.make_async_copy(there, here, sems.at[batches + n]) for n, (there, here) in enumerate(planes)]
    for copy in [later[0]] + copies + later[1:]:
        copy.start()
    each_start()

    @pl.when(is_odd("gx"))
    def _():
        above[...] = rows_partner[...]
        below[...] = rows_other[...]

    @pl.when(~is_odd("gx"))
    def _():
        above[...] = rows_other[...]
        below[...] = rows_partner[...]

    beside_map[...] = beside_matrix()
    spread_winds(winds, above, below)
    kinds = KINDS * LEVELS
    near_up[0:kinds, :] = above[begin * LEVELS : begin * LEVELS + kinds, :].astype(F32)
    near_up[kinds : kinds + 8, :] = jnp.zeros((8, COLS), F32)
    near_down[0:8, :] = jnp.zeros((8, COLS), F32)
    near_down[8 : kinds + 8, :] = below[begin * LEVELS : begin * LEVELS + kinds, :].astype(F32)
    pass_up[kinds : kinds + 8, :] = jnp.zeros((8, COLS), F32)
    pass_down[0:8, :] = jnp.zeros((8, COLS), F32)
    last_row, last_col = at_end("gx"), at_end("gy")
    row16 = lax.broadcasted_iota(jnp.int32, (ROWS, COLS), 0)
    lane16 = lanes((ROWS, COLS))
    row8 = lax.broadcasted_iota(jnp.int32, (8, COLS), 0)
    group = lanes((ROWS, COLS)) // 4

    def packed(start, size):
        kind = lanes((size, COLS)) % 4
        partner, other = from_partner[start : start + size, :].astype(F32), from_other[start : start + size, :].astype(F32)
        theirs = jnp.where((kind < 2) == is_odd("gy"), partner, other)
        return own[start : start + size, :], theirs

    def shifted(centre, first, last):
        up = jnp.where(row16 == 0, first, pltpu.roll(centre, 1, 0))
        if last is None:
            return up, None
        return up, jnp.where(row16 == ROWS - 1, last, pltpu.roll(centre, ROWS - 1, 0))

    _, rows_first = packed(2 * per_level + 4 * ROWS, 16)
    _, rows_last = packed(2 * per_level + 4 * ROWS + 16, 16)
    _, rows_wind = packed(2 * per_level + 4 * ROWS + 32, 16)
    strip_map = strip_matrix()
    _, east_edges = packed(2 * per_level, 2 * ROWS)
    own_north, north_edges = packed(2 * per_level + 2 * ROWS, 2 * ROWS)
    edge_north[...] = north_edges
    norths = dot(jnp.concatenate([north_edges.astype(BF16), own_north], axis=1), strip_map)
    for b in range(2):
        here = slice(b * ROWS, (b + 1) * ROWS)
        east_up, _ = shifted(east_edges[here], rows_wind[8 * b : 8 * b + 1, :], None)
        coefs = coefficients(east_up, east_edges[here], norths[here, :COLS], north_edges[here])
        mine, theirs = packed(b * per_level + begin * ROWS, SLICE)
        sides = dot(jnp.concatenate([theirs.astype(BF16), mine], axis=1), strip_map)
        for f in range(KINDS):
            part = slice(f * ROWS, (f + 1) * ROWS)
            n = 8 * b + begin + f
            up, down = shifted(theirs[part], rows_first[n : n + 1, :], rows_last[n : n + 1, :])
            at = b * SLICE + f * ROWS
            edge_state[at : at + ROWS, :] = theirs[part]
            edge_pass[at : at + ROWS, :] = combine(coefs, theirs[part], up, down, sides[part, :COLS], sides[part, COLS:])

    later[0].wait()
    for copy in copies:
        copy.wait()
    flat = held.reshape((LEVELS + 2) * SLICE, COLS)

    place = lax.broadcasted_iota(jnp.int32, (LEVELS, COLS), 0)
    at_level = lanes((LEVELS, COLS)) // 4 == place % HALF
    upper = place < HALF

    def spread(rows, n):
        value = jnp.where(upper, rows[n : n + 1, :], rows[8 + n : 9 + n, :])
        return jnp.where(at_level, value, 0.0).astype(BF16)

    def sides_of(values, halo):
        both = jnp.concatenate([values, halo], axis=1)
        return dot(both, beside_map[COLS : 3 * COLS, :])

    def wind_of(kind):
        return winds[kind * LEVELS : (kind + 1) * LEVELS, :]

    def strip(near, far, inner, out, offset, east_before, east_after, north_kind, corner, outward):
        north_here = wind_of(north_kind)
        north_left = sides_of(north_here.astype(BF16), spread(rows_wind, north_kind))[:, :COLS]
        coefs = coefficients(east_before, east_after, north_left, north_here)
        for f in range(KINDS):
            values = near[(begin + f) * LEVELS : (begin + f + 1) * LEVELS, :]
            sides = sides_of(values, spread(corner, begin + f))
            beyond = far[count + (begin + f) * LEVELS : count + (begin + f + 1) * LEVELS, :].astype(F32)
            within = flat[pl.ds(SLICE + f * ROWS + inner, LEVELS, stride=SLICE), :]
            up, down = (beyond, within) if outward else (within, beyond)
            at = offset + f * LEVELS
            out[at : at + LEVELS, :] = combine(coefs, values.astype(F32), up, down, sides[:, :COLS], sides[:, COLS:])

    strip(above, above, 0, pass_up, 0, wind_of(1), wind_of(0), 2, rows_first, True)
    own_last = jnp.where(last_row, 0.0, east[pl.ds(ROWS - 1, LEVELS, stride=ROWS), :])
    strip(below, below, ROWS - 1, pass_down, 8, own_last, wind_of(3), 4, rows_last, False)

    for copy in later[1:]:
        copy.wait()

    def load(moving, at, values, edge, number):
        size = values.shape[0]
        high, low = high_low(values)
        moving[at : at + size, 0:COLS] = high
        moving[at : at + size, COLS : 2 * COLS] = low
        mine = lanes((size, COLS)) // 4 == number
        moving[at : at + size, 2 * COLS : 3 * COLS] = jnp.where(mine, edge, 0.0).astype(BF16)

    def one_batch(step, carried):
        previous, coupling, factor = carried
        b = step // (batches // 2)
        edge_at = pl.ds(pl.multiple_of(b * SLICE, SLICE), SLICE)
        north_at = pl.ds(pl.multiple_of(b * ROWS, ROWS), ROWS)
        first_number = (step % (batches // 2)) * BATCH
        norths = []
        for j in range(BATCH):
            level = step * BATCH + j
            here = flat[pl.ds(pl.multiple_of((level + 1) * SLICE, SLICE), SLICE), :]
            load(moving, j * SLICE, here, edge_state[edge_at, :], first_number + j)
            north_here = north[pl.ds(pl.multiple_of(level * ROWS, ROWS), ROWS), :]
            north_here = jnp.where((lane16 == COLS - 1) & last_col, 0.0, north_here)
            norths.append(north_here)
            load(moving_north, j * ROWS, north_here, edge_north[north_at, :], first_number + j)
        north_left = dot(moving_north[...], beside_map[:, 0:COLS])
        sides = dot(moving[...], beside_map[...])
        coefs = []
        for j in range(BATCH):
            level = step * BATCH + j
            at16 = pl.ds(pl.multiple_of(level * ROWS, ROWS), ROWS)
            east_here = jnp.where((row16 == ROWS - 1) & last_row, 0.0, east[at16, :])
            east_up = jnp.where(row16 == 0, winds[pl.ds(level, 1), :], pltpu.roll(east_here, 1, 0))
            coefs.append(coefficients(east_up, east_here, north_left[j * ROWS : (j + 1) * ROWS], norths[j]))

        def stencil(source, offset, j, level, first, last):
            found = []
            for f in range(KINDS):
                at = offset + f * ROWS
                line = f * LEVELS + level
                place = j * SLICE + f * ROWS
                for half in range(2):
                    r = at + 8 * half
                    here = source[pl.ds(pl.multiple_of(r, 8), 8), :]
                    up = source[pl.ds(r - 1, 8), :]
                    down = source[pl.ds(r + 1, 8), :]
                    if half == 0:
                        up = jnp.where(row8 == 0, first[pl.ds(line, 8), :], up)
                    else:
                        down = jnp.where(row8 == 7, last[pl.ds(line + 1, 8), :], down)
                    part = slice(place + 8 * half, place + 8 * half + 8)
                    mine = tuple(c[8 * half : 8 * half + 8] for c in coefs[j])
                    found.append(combine(mine, here, up, down, sides[part, :COLS], sides[part, COLS:]))
            return jnp.concatenate(found, axis=0)

        for j in range(BATCH):
            level = step * BATCH + j
            value = stencil(flat, (level + 1) * SLICE, j, level, near_up, near_down)
            first_pass[8 + j * SLICE : 8 + (j + 1) * SLICE, :] = value
            load(moving, j * SLICE, value, edge_pass[edge_at, :], first_number + j)
        sides = dot(moving[...], beside_map[...])
        for j in range(BATCH):
            level = step * BATCH + j
            value = stencil(first_pass, 8 + j * SLICE, j, level, pass_up, pass_down)
            at16 = pl.ds(pl.multiple_of(level * ROWS, ROWS), ROWS)
            next_at = pl.ds(pl.multiple_of(jnp.minimum(level, LEVELS - 2) * ROWS, ROWS), ROWS)
            next_coupling = jnp.where(level == LEVELS - 1, 0.0, kappa[next_at, :])
            flipped = 1.0 / (1.0 + coupling + next_coupling - coupling * factor)
            keep = coupling * flipped
            factor = next_coupling * flipped
            ratio[at16, :] = factor
            coupling = next_coupling
            after = []
            for f in range(KINDS):
                rhs = value[f * ROWS : (f + 1) * ROWS] * flipped + keep * previous[f]
                flat[pl.ds(pl.multiple_of((level + 1) * SLICE + f * ROWS, ROWS), ROWS), :] = rhs
                after.append(rhs)
            previous = tuple(after)
        return previous, coupling, factor

    start = tuple(jnp.zeros((ROWS, COLS), F32) for _ in range(KINDS))
    first_pass[0:8, :] = jnp.zeros((8, COLS), F32)
    first_pass[8 + BATCH * SLICE : 16 + BATCH * SLICE, :] = jnp.zeros((8, COLS), F32)
    zero = jnp.zeros((ROWS, COLS), F32)
    lax.fori_loop(0, batches, one_batch, (start, zero, zero))

    found = start
    for n in reversed(range(batches)):

        def upward(step, found):
            level = (n + 1) * BATCH - 1 - step
            factor = ratio[pl.ds(pl.multiple_of(level * ROWS, ROWS), ROWS), :]
            after = []
            for f in range(KINDS):
                here = pl.ds(pl.multiple_of((level + 1) * SLICE + f * ROWS, ROWS), ROWS)
                value = flat[here, :] + factor * found[f]
                flat[here, :] = value
                after.append(value)
            return tuple(after)

        found = lax.fori_loop(0, BATCH, upward, found, unroll=UNROLL)
        each_batch(n)


def advance_scratch():
    rows = LEVELS * KINDS + 8
    return [
        pltpu.VMEM((ROW_MESSAGE, COLS), BF16),
        pltpu.VMEM((ROW_MESSAGE, COLS), BF16),
        pltpu.VMEM((LEVELS + 2, SLICE, COLS), F32),
        pltpu.VMEM((8 * LEVELS, COLS), F32),
        pltpu.VMEM((rows, COLS), F32),
        pltpu.VMEM((rows, COLS), F32),
        pltpu.VMEM((rows, COLS), F32),
        pltpu.VMEM((rows, COLS), F32),
        pltpu.VMEM((2 * SLICE, COLS), F32),
        pltpu.VMEM((2 * SLICE, COLS), F32),
        pltpu.VMEM((2 * ROWS, COLS), F32),
        pltpu.VMEM((16 + BATCH * SLICE, COLS), F32),
        pltpu.VMEM((BATCH * SLICE, 3 * COLS), BF16),
        pltpu.VMEM((BATCH * ROWS, 3 * COLS), BF16),
        pltpu.VMEM((3 * COLS, 2 * COLS), BF16),
        pltpu.VMEM((LEVELS * ROWS, COLS), F32),
        pltpu.VMEM((LEVELS * ROWS, COLS), F32),
        pltpu.VMEM(((LEVELS - 1) * ROWS, COLS), F32),
        pltpu.VMEM((LEVELS * ROWS, COLS), F32),
        pltpu.SemaphoreType.DMA((LEVELS // BATCH + 3,)),
    ]


def sigmoid(values):
    return 0.5 * jnp.tanh(0.5 * values) + 0.5


def dot(left, right):
    return jnp.dot(left, right, preferred_element_type=F32)


def dot_last(left, right):
    return lax.dot_general(left, right, (((1,), (1,)), ((), ())), preferred_element_type=F32)


GROUP = 8


def main_kernel(*refs):
    ins, far, (solved, far_adjoint, far_active) = refs[:9], refs[9:15], refs[15:18]
    near, (adjoint, active, sems), scratch = refs[18:24], refs[24:27], refs[27:]
    held = scratch[2]
    fetches = [pltpu.make_async_copy(there, here, sems.at[n]) for n, (there, here) in enumerate(zip(far, near))]
    cotan, w_in_t, w_mid_t, w_out, w_mid, w_in = near
    copies = [
        pltpu.make_async_copy(
            held.at[pl.ds(1 + n * BATCH, BATCH)], solved.at[pl.ds(n * BATCH, BATCH)], sems.at[6 + n]
        )
        for n in range(LEVELS // BATCH)
    ]

    def begin():
        for fetch in fetches:
            fetch.start()

    advance(0, ins, begin, lambda n: copies[n].start(), scratch)
    for fetch in fetches:
        fetch.wait()
    lines = held.reshape((LEVELS + 2) * SLICE, COLS)
    to_slab = ones_where((COLS, COLS), lambda row, col: row == (col % 16) * 8 + col // 16)
    to_physics = ones_where((COLS, COLS), lambda row, col: col == (row % 16) * 8 + row // 16)
    sends = []
    for step in range(ROWS // GROUP):
        rows = [GROUP * step + k for k in range(GROUP)]
        parts = [lines[pl.ds(SLICE + r, FEATURES, stride=ROWS), :].astype(BF16) for r in rows]
        inputs = jnp.concatenate(parts, axis=1)
        first = dot(w_in_t[...], inputs)
        gate = sigmoid(first)
        value = first * gate
        slope_one = gate * (1.0 + first - value)
        second = dot(w_mid_t[...], value.astype(BF16))
        gate = sigmoid(second)
        value = second * gate
        slope_two = gate * (1.0 + second - value)
        here = pl.ds(step * HIDDEN, HIDDEN)
        active[here, :] = value.astype(BF16)
        sends.append(pltpu.make_async_copy(active.at[here], far_active.at[here], sems.at[10 + 2 * step]))
        sends[-1].start()
        blocks = [slice(r * COLS, (r + 1) * COLS) for r in rows]
        moved = jnp.concatenate([dot(to_slab, cotan[at, :]).astype(BF16) for at in blocks], axis=0)
        delta_two = (dot_last(w_out[...], moved) * slope_two).astype(BF16)
        delta_one = (dot(w_mid[...], delta_two) * slope_one).astype(BF16)
        back = dot(w_in[...], delta_one).astype(BF16)
        for k, at in enumerate(blocks):
            adjoint[at, :] = dot_last(to_physics, back[:, k * COLS : (k + 1) * COLS]).astype(BF16)
        here = pl.ds(step * GROUP * COLS, GROUP * COLS)
        sends.append(pltpu.make_async_copy(adjoint.at[here], far_adjoint.at[here], sems.at[11 + 2 * step]))
        sends[-1].start()
    for copy in copies + sends:
        copy.wait()


def last_kernel(*refs):
    ins, (solved, active, w_out_t), out, (mixed, sems), scratch = refs[:9], refs[9:12], refs[12], refs[13:15], refs[15:]
    held = scratch[2]
    batches = LEVELS // BATCH
    fetch = pltpu.make_async_copy(solved, mixed, sems.at[batches + 1])
    fetch.start()
    lines = mixed.reshape(LEVELS * SLICE, COLS)
    for step in range(ROWS // GROUP):
        tend = dot(w_out_t[...], active[step * HIDDEN : (step + 1) * HIDDEN, :])
        tend = tend.astype(BF16).astype(F32)
        if step == 0:
            fetch.wait()
        for k in range(GROUP):
            here = pl.ds(GROUP * step + k, FEATURES, stride=ROWS)
            lines[here, :] = lines[here, :] + tend[:, k * COLS : (k + 1) * COLS]
    first = pltpu.make_async_copy(mixed, out.at[:, pl.ds(0, SLICE), :], sems.at[batches])
    first.start()
    copies = [
        pltpu.make_async_copy(
            held.at[pl.ds(1 + n * BATCH, BATCH)],
            out.at[pl.ds(n * BATCH, BATCH), pl.ds(SLICE, SLICE), :],
            sems.at[n],
        )
        for n in range(batches)
    ]
    advance(KINDS, ins, lambda: None, lambda n: copies[n].start(), scratch)
    first.wait()
    for copy in copies:
        copy.wait()


def run(kernel, outs, scratch, flops, moved, *args, name=None, far=(), limit=62914560, **rest):
    anywhere, near = pl.BlockSpec(memory_space=pl.ANY), pl.BlockSpec(memory_space=pltpu.VMEM)
    rest = rest or dict(in_specs=[anywhere if n in far else near for n in range(len(args))])
    return pl.pallas_call(
        kernel,
        out_shape=[jax.ShapeDtypeStruct(shape, kind) for shape, kind in outs],
        scratch_shapes=scratch,
        compiler_params=pltpu.CompilerParams(vmem_limit_bytes=limit),
        cost_estimate=pl.CostEstimate(flops=flops, bytes_accessed=moved, transcendentals=0),
        name=name,
        **rest,
    )(*args)


FAR = (0, 1, 2, 3)


def main(ins, cotan, *weights):
    near = pl.BlockSpec(memory_space=pltpu.VMEM)
    far = pl.BlockSpec(memory_space=pl.ANY)
    outs = [
        ((LEVELS, SLICE, COLS), F32),
        ((ROWS * COLS, FEATURES), BF16),
        ((ROWS // GROUP * HIDDEN, GROUP * COLS), BF16),
    ]
    held = [pltpu.VMEM(x.shape, BF16) for x in (cotan,) + weights]
    held += [pltpu.VMEM(*outs[1]), pltpu.VMEM(*outs[2]), pltpu.SemaphoreType.DMA((10 + 2 * ROWS // GROUP,))]
    return run(
        main_kernel, outs, held + advance_scratch(), 4 * 10**9, 10**7, *ins, cotan, *weights, name="main",
        in_specs=[far if n in FAR or n >= 9 else near for n in range(15)], out_specs=[far] * 3,
    )


def last(ins, solved, active, w_out_t):
    near = pl.BlockSpec(memory_space=pltpu.VMEM)
    far = pl.BlockSpec(memory_space=pl.ANY)
    mixed = [pltpu.VMEM((LEVELS, SLICE, COLS), F32), pltpu.SemaphoreType.DMA((LEVELS // BATCH + 2,))]
    (new_state,) = run(
        last_kernel, [((LEVELS, FIELDS * ROWS, COLS), F32)], mixed + advance_scratch(), 10**9, 2 * 10**7,
        *ins, solved, active, w_out_t, name="last_fields",
        in_specs=[far if n in FAR + (9,) else near for n in range(12)], out_specs=[far],
    )
    return new_state


def swap(block, axis, start):
    firsts = range(start, lax.axis_size(axis) - 1, 2)
    return lax.ppermute(block, axis, [(i, i + 1) for i in firsts] + [(i + 1, i) for i in firsts])


def exchange(blocks):
    return lax.all_to_all(blocks, ("gx", "gy"), split_axis=0, concat_axis=0, tiled=True)


def shards(state, east_wind, north_wind, kappa, w_in, w_mid, w_out, cotangent):
    devices = lax.axis_size("gx") * lax.axis_size("gy")
    flat = state.reshape(LEVELS * FIELDS * ROWS, COLS)
    east = east_wind.reshape(LEVELS * ROWS, COLS)
    north = north_wind.reshape(LEVELS * ROWS, COLS)
    message = ((ROW_MESSAGE, COLS), BF16)
    to_partner, to_other = run(rows_kernel, [message, message], [], 10**6, 5 * 10**6, flat, east, north, name="rows")
    arrived = exchange(cotangent.reshape(devices, ROWS * COLS // devices, FEATURES))
    from_other = swap(to_other, "gx", 1)
    from_partner = swap(to_partner, "gx", 0)
    count = LEVELS * FIELDS
    flipped = [(w.shape[::-1], BF16) for w in (w_in, w_mid, w_out)]
    edges, w_in_t, w_mid_t, w_out_t = run(
        cols_kernel, [((COL_MESSAGE - 48, COLS), BF16)] + flipped, [], 10**8, 10**7,
        flat, east, north, w_in, w_mid, w_out, name="cols",
    )
    (own,) = run(
        corners_kernel, [((COL_MESSAGE, COLS), BF16)], [pltpu.VMEM((count, COLS), BF16)], 10**6, 10**6,
        edges, from_partner, from_other, name="corners", limit=8 * 1024 * 1024,
    )
    rows_partner, rows_other = from_partner, from_other
    from_other = swap(own, "gy", 1)
    from_partner = swap(own, "gy", 0)
    ins = (state.reshape(LEVELS, FIELDS * ROWS, COLS), east, north, kappa.reshape((LEVELS - 1) * ROWS, COLS))
    ins += (rows_partner, rows_other, own, from_partner, from_other)
    cotan = arrived.reshape(ROWS * COLS, FEATURES)
    solved, adjoint, active = main(ins, cotan, w_in_t, w_mid_t, w_out, w_mid, w_in)
    returned = exchange(adjoint.reshape(devices, ROWS * COLS // devices, FEATURES))
    new_state = last(ins, solved, active, w_out_t)
    return new_state.reshape(state.shape), returned.reshape(ROWS * COLS, FEATURES)


def solution(mesh):
    in_specs = (
        P(None, None, "gx", "gy"),
        P(None, "gx", "gy"),
        P(None, "gx", "gy"),
        P(None, "gx", "gy"),
        P(),
        P(),
        P(),
        P(("gx", "gy"), None),
    )
    out_specs = (P(None, None, "gx", "gy"), P(("gx", "gy"), None))
    return jax.shard_map(shards, mesh=mesh, in_specs=in_specs, out_specs=out_specs, check_vma=False)
```

profile of v0, /device:TPU:1, one launch (start us, length us, event | category | flops | bytes accessed | tf_op | source)
XLA Modules:
  0.0 84.8 jit_solution(14906348565126004102)
XLA Ops:
  0.6 11.5 %all-to-all-start = ((bf16[128,16,256]{2,1,0:T(8,128)(2,1)}), bf16[128,16,256]{2,1,0:T(8,128)(2,1)S(1)}, u32[]{:S(2)}, u32[]{:S(2)}) async-start(bf16[128,16,256]{2,1,0:T(8,128)(2,1)} %bitcast.24), calls=%async_computation | async-start | bytes 2097152 | tf_op jit(solution)/shard_map/all_to_all | solution.py:595
  12.1 3.9 %rows.1 = (bf16[1216,128]{1,0:T(8,128)(2,1)}, bf16[1216,128]{1,0:T(8,128)(2,1)}) custom-call(f32[8192,128]{1,0:T(8,128)} %bitcast.10, f32[1024,128]{1,0:T(8,128)} %bitcast.14, f32[1024,128]{1,0:T(8,128)} %bitcast.18), custom_call_target="tpu_custom_call" | custom-call | flops 1000000 | bytes 5000000 | tf_op jit(solution)/shard_map/rows/pallas_call | solution.py:547
  16.1 1.1 %collective-permute-start = (bf16[1216,128]{1,0:T(8,128)(2,1)}, bf16[1216,128]{1,0:T(8,128)(2,1)S(1)}, u32[]{:S(2)}, u32[]{:S(2)}) collective-permute-start(bf16[1216,128]{1,0:T(8,128)(2,1)} %get-tuple-element.11), channel_id=1, source_target_pairs={{0,8},{16,24},{32,40},{48,56},{64,72},{80,88},{96,104},{112,120},{... | collective-permute-start | bytes 933896 | tf_op jit(solution)/shard_map/ppermute | solution.py:591
  17.1 2.6 %collective-permute-start.1 = (bf16[1216,128]{1,0:T(8,128)(2,1)}, bf16[1216,128]{1,0:T(8,128)(2,1)S(1)}, u32[]{:S(2)}, u32[]{:S(2)}) collective-permute-start(bf16[1216,128]{1,0:T(8,128)(2,1)} %get-tuple-element.12), channel_id=1, source_target_pairs={{8,16},{24,32},{40,48},{56,64},{72,80},{88,96},{104,112},{16,8},{3... | collective-permute-start | bytes 933896 | tf_op jit(solution)/shard_map/ppermute | solution.py:591
  19.8 5.2 %cols.1 = (bf16[320,128]{1,0:T(8,128)(2,1)}, bf16[512,256]{1,0:T(8,128)(2,1)}, bf16[512,512]{1,0:T(8,128)(2,1)}, bf16[256,512]{1,0:T(8,128)(2,1)}) custom-call(f32[8192,128]{1,0:T(8,128)} %bitcast.11, f32[1024,128]{1,0:T(8,128)} %bitcast.15, f32[1024,128]{1,0:T(8,128)} %bitcast.19, bf16[256,512]{1,0:T(8,128)(2,1)} %refs_14_.1, bf16[512,512]{1,0:T(8,128)(2,1)} %refs_13_.1, ...), custom_call_target="tpu_custom_call" | custom-call | flops 100000000 | bytes 10000000 | tf_op jit(solution)/shard_map/cols/pallas_call | solution.py:547
  25.0 0.0 collective-permute-done.from_partner.refs_4_
  25.0 0.0 copy-start
  25.0 3.7 %collective-permute-done.1.from_other.refs_5_ = bf16[1216,128]{1,0:T(8,128)(2,1)S(1)} collective-permute-done((bf16[1216,128]{1,0:T(8,128)(2,1)}, bf16[1216,128]{1,0:T(8,128)(2,1)S(1)}, u32[]{:S(2)}, u32[]{:S(2)}) %collective-permute-start.1) | collective-permute-done | bytes 311328 | tf_op jit(solution)/shard_map/ppermute | solution.py:591
  28.7 0.0 copy-start.1
  28.7 0.0 copy-start.3
  28.7 1.0 %copy-done.3 = bf16[320,128]{1,0:T(8,128)(2,1)S(1)} copy-done((bf16[320,128]{1,0:T(8,128)(2,1)S(1)}, bf16[320,128]{1,0:T(8,128)(2,1)}, u32[]{:S(2)}) %copy-start.3) | copy-done | bytes 81944
  29.6 0.7 corners.1.refs_6_
  30.3 0.0 copy-start.2
  30.4 0.7 collective-permute-start.3
  31.0 3.7 %collective-permute-start.2 = (bf16[368,128]{1,0:T(8,128)(2,1)S(1)}, bf16[368,128]{1,0:T(8,128)(2,1)S(1)}, u32[]{:S(2)}, u32[]{:S(2)}) collective-permute-start(bf16[368,128]{1,0:T(8,128)(2,1)S(1)} %corners.1.refs_6_), channel_id=1, source_target_pairs={{0,1},{2,3},{4,5},{6,7},{1,0},{3,2},{5,4},{7,6},{8,9},{10,11},{12,... | collective-permute-start | bytes 282632 | tf_op jit(solution)/shard_map/ppermute | solution.py:591
  34.7 0.0 collective-permute-done.3.refs_8_
  34.7 0.0 copy-start.5
  34.7 2.0 %collective-permute-done.2.refs_7_ = bf16[368,128]{1,0:T(8,128)(2,1)S(1)} collective-permute-done((bf16[368,128]{1,0:T(8,128)(2,1)S(1)}, bf16[368,128]{1,0:T(8,128)(2,1)S(1)}, u32[]{:S(2)}, u32[]{:S(2)}) %collective-permute-start.2) | collective-permute-done | bytes 94240 | tf_op jit(solution)/shard_map/ppermute | solution.py:591
  36.7 0.0 copy-start.6
  36.7 0.0 all-to-all-done
  36.7 0.0 copy-start.4
  36.7 0.0 copy-done
  36.7 0.0 copy-done.1
  36.7 0.0 copy-done.2
  36.7 0.0 copy-done.5
  36.7 0.6 copy-done.6
  37.3 0.4 copy-done.4
  37.7 16.0 %main.1 = (f32[64,64,128]{2,1,0:T(8,128)}, bf16[2048,256]{1,0:T(8,128)(2,1)}, bf16[1024,1024]{1,0:T(8,128)(2,1)}) custom-call(f32[64,128,128]{2,1,0:T(8,128)} %bitcast.12, f32[1024,128]{1,0:T(8,128)} %bitcast.16, f32[1024,128]{1,0:T(8,128)} %bitcast.20, f32[1008,128]{1,0:T(8,128)} %bitcast.27, bf16[1216,128]{1,0:T(8,128)(2,1)} %copy-done, ...), custom_call_target="tpu_custom_call" | custom-call | flops 4000000000 | bytes 10000000 | tf_op jit(solution)/shard_map/main/pallas_call | solution.py:547
  53.7 11.2 %all-to-all-start.1 = ((bf16[128,16,256]{2,1,0:T(8,128)(2,1)}), bf16[128,16,256]{2,1,0:T(8,128)(2,1)S(1)}, u32[]{:S(2)}, u32[]{:S(2)}) async-start(bf16[128,16,256]{2,1,0:T(8,128)(2,1)} %bitcast.26), calls=%async_computation.1 | async-start | bytes 2097152 | tf_op jit(solution)/shard_map/all_to_all | solution.py:595
  65.0 12.3 %last_fields.1 = f32[64,128,128]{2,1,0:T(8,128)} custom-call(f32[64,128,128]{2,1,0:T(8,128)} %bitcast.13, f32[1024,128]{1,0:T(8,128)} %bitcast.17, f32[1024,128]{1,0:T(8,128)} %bitcast.21, f32[1008,128]{1,0:T(8,128)} %bitcast.28, bf16[1216,128]{1,0:T(8,128)(2,1)} %copy-done, bf16[1216,128]{1,0:T(8,128)(2,1)} %copy-done.1, bf16[368,128]{1,0:T(8,128)(2,1)} %copy-done.2, ...), custom_call_target="tpu_custom_call" | custom-call | flops 1000000000 | bytes 20000000 | tf_op jit(solution)/shard_map/last_fields/pallas_call | solution.py:547
  77.2 6.6 %all-to-all-done.1 = bf16[128,16,256]{2,1,0:T(8,128)(2,1)S(1)} async-done(((bf16[128,16,256]{2,1,0:T(8,128)(2,1)}), bf16[128,16,256]{2,1,0:T(8,128)(2,1)S(1)}, u32[]{:S(2)}, u32[]{:S(2)}) %all-to-all-start.1) | async-done | bytes 1048608 | tf_op jit(solution)/shard_map/all_to_all | solution.py:595
  83.9 1.0 %copy.11 = bf16[2048,256]{1,0:T(8,128)(2,1)} copy(bf16[2048,256]{1,0:T(8,128)(2,1)S(1)} %bitcast.22) | data formatting | bytes 2097152
Async XLA Ops:
  0.6 36.1 %all-to-all-start = ((bf16[128,16,256]{2,1,0:T(8,128)(2,1)}), bf16[128,16,256]{2,1,0:T(8,128)(2,1)S(1)}, u32[]{:S(2)}, u32[]{:S(2)}) async-start(bf16[128,16,256]{2,1,0:T(8,128)(2,1)} %bitcast.24), calls=%async_computation | async-start | bytes 2097152 | tf_op jit(solution)/shard_map/all_to_all | solution.py:595
  16.1 8.9 %collective-permute-start = (bf16[1216,128]{1,0:T(8,128)(2,1)}, bf16[1216,128]{1,0:T(8,128)(2,1)S(1)}, u32[]{:S(2)}, u32[]{:S(2)}) collective-permute-start(bf16[1216,128]{1,0:T(8,128)(2,1)} %get-tuple-element.11), channel_id=1, source_target_pairs={{0,8},{16,24},{32,40},{48,56},{64,72},{80,88},{96,104},{112,120},{... | collective-permute-start | bytes 933896 | tf_op jit(solution)/shard_map/ppermute | solution.py:591
  17.1 11.5 %collective-permute-start.1 = (bf16[1216,128]{1,0:T(8,128)(2,1)}, bf16[1216,128]{1,0:T(8,128)(2,1)S(1)}, u32[]{:S(2)}, u32[]{:S(2)}) collective-permute-start(bf16[1216,128]{1,0:T(8,128)(2,1)} %get-tuple-element.12), channel_id=1, source_target_pairs={{8,16},{24,32},{40,48},{56,64},{72,80},{88,96},{104,112},{16,8},{3... | collective-permute-start | bytes 933896 | tf_op jit(solution)/shard_map/ppermute | solution.py:591
  25.0 11.7 %copy-start = (bf16[1216,128]{1,0:T(8,128)(2,1)}, bf16[1216,128]{1,0:T(8,128)(2,1)S(1)}, u32[]{:S(2)}) copy-start(bf16[1216,128]{1,0:T(8,128)(2,1)S(1)} %collective-permute-done.from_partner.refs_4_) | copy-start | bytes 933892
  28.7 8.0 %copy-start.1 = (bf16[1216,128]{1,0:T(8,128)(2,1)}, bf16[1216,128]{1,0:T(8,128)(2,1)S(1)}, u32[]{:S(2)}) copy-start(bf16[1216,128]{1,0:T(8,128)(2,1)S(1)} %collective-permute-done.1.from_other.refs_5_) | copy-start | bytes 933892
  28.7 1.0 %copy-start.3 = (bf16[320,128]{1,0:T(8,128)(2,1)S(1)}, bf16[320,128]{1,0:T(8,128)(2,1)}, u32[]{:S(2)}) copy-start(bf16[320,128]{1,0:T(8,128)(2,1)} %get-tuple-element.13.edges) | copy-start | bytes 245764
  30.3 6.4 %copy-start.2 = (bf16[368,128]{1,0:T(8,128)(2,1)}, bf16[368,128]{1,0:T(8,128)(2,1)S(1)}, u32[]{:S(2)}) copy-start(bf16[368,128]{1,0:T(8,128)(2,1)S(1)} %corners.1.refs_6_) | copy-start | bytes 282628
  30.4 4.4 %collective-permute-start.3 = (bf16[368,128]{1,0:T(8,128)(2,1)S(1)}, bf16[368,128]{1,0:T(8,128)(2,1)S(1)}, u32[]{:S(2)}, u32[]{:S(2)}) collective-permute-start(bf16[368,128]{1,0:T(8,128)(2,1)S(1)} %corners.1.refs_6_), channel_id=1, source_target_pairs={{1,2},{3,4},{5,6},{2,1},{4,3},{6,5},{9,10},{11,12},{13,14},{10,9},... | collective-permute-start | bytes 282632 | tf_op jit(solution)/shard_map/ppermute | solution.py:591
  31.0 5.7 %collective-permute-start.2 = (bf16[368,128]{1,0:T(8,128)(2,1)S(1)}, bf16[368,128]{1,0:T(8,128)(2,1)S(1)}, u32[]{:S(2)}, u32[]{:S(2)}) collective-permute-start(bf16[368,128]{1,0:T(8,128)(2,1)S(1)} %corners.1.refs_6_), channel_id=1, source_target_pairs={{0,1},{2,3},{4,5},{6,7},{1,0},{3,2},{5,4},{7,6},{8,9},{10,11},{12,... | collective-permute-start | bytes 282632 | tf_op jit(solution)/shard_map/ppermute | solution.py:591
  34.7 2.0 %copy-start.5 = (bf16[368,128]{1,0:T(8,128)(2,1)}, bf16[368,128]{1,0:T(8,128)(2,1)S(1)}, u32[]{:S(2)}) copy-start(bf16[368,128]{1,0:T(8,128)(2,1)S(1)} %collective-permute-done.3.refs_8_) | copy-start | bytes 282628
  36.7 0.6 copy-start.6
  36.7 1.0 %copy-start.4 = (bf16[128,16,256]{2,1,0:T(8,128)(2,1)}, bf16[128,16,256]{2,1,0:T(8,128)(2,1)S(1)}, u32[]{:S(2)}) copy-start(bf16[128,16,256]{2,1,0:T(8,128)(2,1)S(1)} %all-to-all-done) | copy-start | bytes 3145732
  53.7 30.2 %all-to-all-start.1 = ((bf16[128,16,256]{2,1,0:T(8,128)(2,1)}), bf16[128,16,256]{2,1,0:T(8,128)(2,1)S(1)}, u32[]{:S(2)}, u32[]{:S(2)}) async-start(bf16[128,16,256]{2,1,0:T(8,128)(2,1)} %bitcast.26), calls=%async_computation.1 | async-start | bytes 2097152 | tf_op jit(solution)/shard_map/all_to_all | solution.py:595
where the time goes:
time: 85.2 us; the launch traced here: 84.8 us
  Pallas kernels  38.2 us (45%)
  starting transfers between devices  30.8 us (36%)
  waiting for transfers between devices  12.3 us (14%)
  local copies, waits for them, and re-layouts  2.9 us (3%)
    pallas_call x5, Pallas kernels, run(): pl.pallas_call(kernel, out_shape=[jax.ShapeDtypeStruct(shape, kind) for s...  38.2 us
    all_to_all x2, starting transfers between devices, exchange(): lax.all_to_all(blocks, ('gx', 'gy'), split_axis=0, concat_axis=0, tiled=T...  22.7 us
    ppermute x4, starting transfers between devices, swap(): lax.ppermute(block, axis, [(i, i + 1) for i in firsts] + [(i + 1, i) for...  8.04 us
    all_to_all x2, waiting for transfers between devices, exchange(): lax.all_to_all(blocks, ('gx', 'gy'), split_axis=0, concat_axis=0, tiled=T...  6.64 us
    ppermute x4, waiting for transfers between devices, swap(): lax.ppermute(block, axis, [(i, i + 1) for i in firsts] + [(i + 1, i) for...  5.64 us
    unnamed x15, local copies, waits for them, and re-layouts  2.9 us
  transfers between devices with their start and end apart: 6, of which 3 were waited for; matrix products, arithmetic and copies ran while one was open for 0% of the time, Pallas kernels for 26%

commit v1 on v0

--- a/solution.py
+++ b/solution.py
@@ -163,9 +163,9 @@
         lane, place = row % COLS, col % COLS
         inside = either(col < COLS, lane + 1 == place, lane == place + 1)
         halo = either(col < COLS, (place == 0) & (lane % 4 == 1), (place == COLS - 1) & (lane % 4 == 2))
-        return either(row < 2 * COLS, inside, halo)
-
-    return ones_where((3 * COLS, 2 * COLS), rule)
+        return either(row < COLS, inside, halo)
+
+    return ones_where((2 * COLS, 2 * COLS), rule)
 
 
 def strip_matrix():
@@ -182,11 +182,6 @@
 
 def either(choice, yes, no):
     return (choice & yes) | (~choice & no)
-
-
-def high_low(values):
-    high = values.astype(BF16)
-    return high, (values - high.astype(F32)).astype(BF16)
 
 
 BATCH = 32
@@ -288,7 +283,7 @@
 
     def sides_of(values, halo):
         both = jnp.concatenate([values, halo], axis=1)
-        return dot(both, beside_map[COLS : 3 * COLS, :])
+        return dot(both, beside_map[...])
 
     def wind_of(kind):
         return winds[kind * LEVELS : (kind + 1) * LEVELS, :]
@@ -315,11 +310,9 @@
 
     def load(moving, at, values, edge, number):
         size = values.shape[0]
-        high, low = high_low(values)
-        moving[at : at + size, 0:COLS] = high
-        moving[at : at + size, COLS : 2 * COLS] = low
         mine = lanes((size, COLS)) // 4 == number
-        moving[at : at + size, 2 * COLS : 3 * COLS] = jnp.where(mine, edge, 0.0).astype(BF16)
+        moving[at : at + size, 0:COLS] = values.astype(BF16)
+        moving[at : at + size, COLS : 2 * COLS] = jnp.where(mine, edge, 0.0).astype(BF16)
 
     def one_batch(step, carried):
         previous, coupling, factor = carried
@@ -430,9 +423,9 @@
         pltpu.VMEM((2 * SLICE, COLS), F32),
         pltpu.VMEM((2 * ROWS, COLS), F32),
         pltpu.VMEM((16 + BATCH * SLICE, COLS), F32),
-        pltpu.VMEM((BATCH * SLICE, 3 * COLS), BF16),
-        pltpu.VMEM((BATCH * ROWS, 3 * COLS), BF16),
-        pltpu.VMEM((3 * COLS, 2 * COLS), BF16),
+        pltpu.VMEM((BATCH * SLICE, 2 * COLS), BF16),
+        pltpu.VMEM((BATCH * ROWS, 2 * COLS), BF16),
+        pltpu.VMEM((2 * COLS, 2 * COLS), BF16),
         pltpu.VMEM((LEVELS * ROWS, COLS), F32),
         pltpu.VMEM((LEVELS * ROWS, COLS), F32),
         pltpu.VMEM(((LEVELS - 1) * ROWS, COLS), F32),

time: 85.2 us -> 84 us (0.986)
  Pallas kernels: 38.2 us -> 35.4 us
  waiting for transfers between devices: 12.3 us -> 13.8 us
    pallas_call x5, Pallas kernels: 38.2 us -> 35.4 us  [run(): pl.pallas_call(kernel, out_shape=[jax.ShapeDtypeStruct(shape, kind) for s...]
    all_to_all x2, waiting for transfers between devices: 6.64 us -> 8.13 us  [exchange(): lax.all_to_all(blocks, ('gx', 'gy'), split_axis=0, concat_axis=0, tiled=T...]
  transfers between devices with their start and end apart: 6 -> 6, of which waited for: 3 -> 3; matrix products, arithmetic and copies ran while one was open for 0% -> 0% of each run, Pallas kernels for 26% -> 25%
where the time goes in v1:
time: 84 us; the launch traced here: 83.6 us
  Pallas kernels  35.4 us (42%)
  starting transfers between devices  30.8 us (37%)
  waiting for transfers between devices  13.8 us (16%)
  local copies, waits for them, and re-layouts  2.9 us (3%)
    pallas_call x5, Pallas kernels, run(): pl.pallas_call(kernel, out_shape=[jax.ShapeDtypeStruct(shape, kind) for s...  35.4 us
    all_to_all x2, starting transfers between devices, exchange(): lax.all_to_all(blocks, ('gx', 'gy'), split_axis=0, concat_axis=0, tiled=T...  22.7 us
    all_to_all x2, waiting for transfers between devices, exchange(): lax.all_to_all(blocks, ('gx', 'gy'), split_axis=0, concat_axis=0, tiled=T...  8.13 us
    ppermute x4, starting transfers between devices, swap(): lax.ppermute(block, axis, [(i, i + 1) for i in firsts] + [(i + 1, i) for...  8.04 us
    ppermute x4, waiting for transfers between devices, swap(): lax.ppermute(block, axis, [(i, i + 1) for i in firsts] + [(i + 1, i) for...  5.64 us
    unnamed x15, local copies, waits for them, and re-layouts  2.9 us
  transfers between devices with their start and end apart: 6, of which 3 were waited for; matrix products, arithmetic and copies ran while one was open for 0% of the time, Pallas kernels for 25%

profile of v1, /device:TPU:1, one launch (start us, length us, event | category | flops | bytes accessed | tf_op | source)
XLA Modules:
  0.0 83.6 jit_solution(12048529125905212253)
XLA Ops:
  0.6 11.5 %all-to-all-start = ((bf16[128,16,256]{2,1,0:T(8,128)(2,1)}), bf16[128,16,256]{2,1,0:T(8,128)(2,1)S(1)}, u32[]{:S(2)}, u32[]{:S(2)}) async-start(bf16[128,16,256]{2,1,0:T(8,128)(2,1)} %bitcast.24), calls=%async_computation | async-start | bytes 2097152 | tf_op jit(solution)/shard_map/all_to_all | solution.py:588
  12.1 3.9 %rows.1 = (bf16[1216,128]{1,0:T(8,128)(2,1)}, bf16[1216,128]{1,0:T(8,128)(2,1)}) custom-call(f32[8192,128]{1,0:T(8,128)} %bitcast.10, f32[1024,128]{1,0:T(8,128)} %bitcast.14, f32[1024,128]{1,0:T(8,128)} %bitcast.18), custom_call_target="tpu_custom_call" | custom-call | flops 1000000 | bytes 5000000 | tf_op jit(solution)/shard_map/rows/pallas_call | solution.py:540
  16.1 1.1 %collective-permute-start = (bf16[1216,128]{1,0:T(8,128)(2,1)}, bf16[1216,128]{1,0:T(8,128)(2,1)S(1)}, u32[]{:S(2)}, u32[]{:S(2)}) collective-permute-start(bf16[1216,128]{1,0:T(8,128)(2,1)} %get-tuple-element.11), channel_id=1, source_target_pairs={{0,8},{16,24},{32,40},{48,56},{64,72},{80,88},{96,104},{112,120},{... | collective-permute-start | bytes 933896 | tf_op jit(solution)/shard_map/ppermute | solution.py:584
  17.1 2.6 %collective-permute-start.1 = (bf16[1216,128]{1,0:T(8,128)(2,1)}, bf16[1216,128]{1,0:T(8,128)(2,1)S(1)}, u32[]{:S(2)}, u32[]{:S(2)}) collective-permute-start(bf16[1216,128]{1,0:T(8,128)(2,1)} %get-tuple-element.12), channel_id=1, source_target_pairs={{8,16},{24,32},{40,48},{56,64},{72,80},{88,96},{104,112},{16,8},{3... | collective-permute-start | bytes 933896 | tf_op jit(solution)/shard_map/ppermute | solution.py:584
  19.8 5.2 %cols.1 = (bf16[320,128]{1,0:T(8,128)(2,1)}, bf16[512,256]{1,0:T(8,128)(2,1)}, bf16[512,512]{1,0:T(8,128)(2,1)}, bf16[256,512]{1,0:T(8,128)(2,1)}) custom-call(f32[8192,128]{1,0:T(8,128)} %bitcast.11, f32[1024,128]{1,0:T(8,128)} %bitcast.15, f32[1024,128]{1,0:T(8,128)} %bitcast.19, bf16[256,512]{1,0:T(8,128)(2,1)} %refs_14_.1, bf16[512,512]{1,0:T(8,128)(2,1)} %refs_13_.1, ...), custom_call_target="tpu_custom_call" | custom-call | flops 100000000 | bytes 10000000 | tf_op jit(solution)/shard_map/cols/pallas_call | solution.py:540
  25.0 0.0 collective-permute-done.from_partner.refs_4_
  25.0 0.0 copy-start
  25.0 3.7 %collective-permute-done.1.from_other.refs_5_ = bf16[1216,128]{1,0:T(8,128)(2,1)S(1)} collective-permute-done((bf16[1216,128]{1,0:T(8,128)(2,1)}, bf16[1216,128]{1,0:T(8,128)(2,1)S(1)}, u32[]{:S(2)}, u32[]{:S(2)}) %collective-permute-start.1) | collective-permute-done | bytes 311328 | tf_op jit(solution)/shard_map/ppermute | solution.py:584
  28.7 0.0 copy-start.1
  28.7 0.0 copy-start.3
  28.7 1.0 %copy-done.3 = bf16[320,128]{1,0:T(8,128)(2,1)S(1)} copy-done((bf16[320,128]{1,0:T(8,128)(2,1)S(1)}, bf16[320,128]{1,0:T(8,128)(2,1)}, u32[]{:S(2)}) %copy-start.3) | copy-done | bytes 81944
  29.6 0.7 corners.1.refs_6_
  30.3 0.0 copy-start.2
  30.4 0.7 collective-permute-start.3
  31.0 3.7 %collective-permute-start.2 = (bf16[368,128]{1,0:T(8,128)(2,1)S(1)}, bf16[368,128]{1,0:T(8,128)(2,1)S(1)}, u32[]{:S(2)}, u32[]{:S(2)}) collective-permute-start(bf16[368,128]{1,0:T(8,128)(2,1)S(1)} %corners.1.refs_6_), channel_id=1, source_target_pairs={{0,1},{2,3},{4,5},{6,7},{1,0},{3,2},{5,4},{7,6},{8,9},{10,11},{12,... | collective-permute-start | bytes 282632 | tf_op jit(solution)/shard_map/ppermute | solution.py:584
  34.7 0.0 collective-permute-done.3.refs_8_
  34.7 0.0 copy-start.5
  34.7 2.0 %collective-permute-done.2.refs_7_ = bf16[368,128]{1,0:T(8,128)(2,1)S(1)} collective-permute-done((bf16[368,128]{1,0:T(8,128)(2,1)S(1)}, bf16[368,128]{1,0:T(8,128)(2,1)S(1)}, u32[]{:S(2)}, u32[]{:S(2)}) %collective-permute-start.2) | collective-permute-done | bytes 94240 | tf_op jit(solution)/shard_map/ppermute | solution.py:584
  36.7 0.0 copy-start.6
  36.7 0.0 all-to-all-done
  36.7 0.0 copy-start.4
  36.7 0.0 copy-done
  36.7 0.0 copy-done.1
  36.7 0.0 copy-done.2
  36.7 0.0 copy-done.5
  36.7 0.6 copy-done.6
  37.3 0.4 copy-done.4
  37.7 14.8 %main.1 = (f32[64,64,128]{2,1,0:T(8,128)}, bf16[2048,256]{1,0:T(8,128)(2,1)}, bf16[1024,1024]{1,0:T(8,128)(2,1)}) custom-call(f32[64,128,128]{2,1,0:T(8,128)} %bitcast.12, f32[1024,128]{1,0:T(8,128)} %bitcast.16, f32[1024,128]{1,0:T(8,128)} %bitcast.20, f32[1008,128]{1,0:T(8,128)} %bitcast.27, bf16[1216,128]{1,0:T(8,128)(2,1)} %copy-done, ...), custom_call_target="tpu_custom_call" | custom-call | flops 4000000000 | bytes 10000000 | tf_op jit(solution)/shard_map/main/pallas_call | solution.py:540
  52.5 11.2 %all-to-all-start.1 = ((bf16[128,16,256]{2,1,0:T(8,128)(2,1)}), bf16[128,16,256]{2,1,0:T(8,128)(2,1)S(1)}, u32[]{:S(2)}, u32[]{:S(2)}) async-start(bf16[128,16,256]{2,1,0:T(8,128)(2,1)} %bitcast.26), calls=%async_computation.1 | async-start | bytes 2097152 | tf_op jit(solution)/shard_map/all_to_all | solution.py:588
  63.7 10.8 %last_fields.1 = f32[64,128,128]{2,1,0:T(8,128)} custom-call(f32[64,128,128]{2,1,0:T(8,128)} %bitcast.13, f32[1024,128]{1,0:T(8,128)} %bitcast.17, f32[1024,128]{1,0:T(8,128)} %bitcast.21, f32[1008,128]{1,0:T(8,128)} %bitcast.28, bf16[1216,128]{1,0:T(8,128)(2,1)} %copy-done, bf16[1216,128]{1,0:T(8,128)(2,1)} %copy-done.1, bf16[368,128]{1,0:T(8,128)(2,1)} %copy-done.2, ...), custom_call_target="tpu_custom_call" | custom-call | flops 1000000000 | bytes 20000000 | tf_op jit(solution)/shard_map/last_fields/pallas_call | solution.py:540
  74.5 8.1 %all-to-all-done.1 = bf16[128,16,256]{2,1,0:T(8,128)(2,1)S(1)} async-done(((bf16[128,16,256]{2,1,0:T(8,128)(2,1)}), bf16[128,16,256]{2,1,0:T(8,128)(2,1)S(1)}, u32[]{:S(2)}, u32[]{:S(2)}) %all-to-all-start.1) | async-done | bytes 1048608 | tf_op jit(solution)/shard_map/all_to_all | solution.py:588
  82.6 1.0 %copy.11 = bf16[2048,256]{1,0:T(8,128)(2,1)} copy(bf16[2048,256]{1,0:T(8,128)(2,1)S(1)} %bitcast.22) | data formatting | bytes 2097152
Async XLA Ops:
  0.6 36.1 %all-to-all-start = ((bf16[128,16,256]{2,1,0:T(8,128)(2,1)}), bf16[128,16,256]{2,1,0:T(8,128)(2,1)S(1)}, u32[]{:S(2)}, u32[]{:S(2)}) async-start(bf16[128,16,256]{2,1,0:T(8,128)(2,1)} %bitcast.24), calls=%async_computation | async-start | bytes 2097152 | tf_op jit(solution)/shard_map/all_to_all | solution.py:588
  16.1 8.9 %collective-permute-start = (bf16[1216,128]{1,0:T(8,128)(2,1)}, bf16[1216,128]{1,0:T(8,128)(2,1)S(1)}, u32[]{:S(2)}, u32[]{:S(2)}) collective-permute-start(bf16[1216,128]{1,0:T(8,128)(2,1)} %get-tuple-element.11), channel_id=1, source_target_pairs={{0,8},{16,24},{32,40},{48,56},{64,72},{80,88},{96,104},{112,120},{... | collective-permute-start | bytes 933896 | tf_op jit(solution)/shard_map/ppermute | solution.py:584
  17.1 11.5 %collective-permute-start.1 = (bf16[1216,128]{1,0:T(8,128)(2,1)}, bf16[1216,128]{1,0:T(8,128)(2,1)S(1)}, u32[]{:S(2)}, u32[]{:S(2)}) collective-permute-start(bf16[1216,128]{1,0:T(8,128)(2,1)} %get-tuple-element.12), channel_id=1, source_target_pairs={{8,16},{24,32},{40,48},{56,64},{72,80},{88,96},{104,112},{16,8},{3... | collective-permute-start | bytes 933896 | tf_op jit(solution)/shard_map/ppermute | solution.py:584
  25.0 11.7 %copy-start = (bf16[1216,128]{1,0:T(8,128)(2,1)}, bf16[1216,128]{1,0:T(8,128)(2,1)S(1)}, u32[]{:S(2)}) copy-start(bf16[1216,128]{1,0:T(8,128)(2,1)S(1)} %collective-permute-done.from_partner.refs_4_) | copy-start | bytes 933892
  28.7 8.0 %copy-start.1 = (bf16[1216,128]{1,0:T(8,128)(2,1)}, bf16[1216,128]{1,0:T(8,128)(2,1)S(1)}, u32[]{:S(2)}) copy-start(bf16[1216,128]{1,0:T(8,128)(2,1)S(1)} %collective-permute-done.1.from_other.refs_5_) | copy-start | bytes 933892
  28.7 1.0 %copy-start.3 = (bf16[320,128]{1,0:T(8,128)(2,1)S(1)}, bf16[320,128]{1,0:T(8,128)(2,1)}, u32[]{:S(2)}) copy-start(bf16[320,128]{1,0:T(8,128)(2,1)} %get-tuple-element.13.edges) | copy-start | bytes 245764
  30.3 6.4 %copy-start.2 = (bf16[368,128]{1,0:T(8,128)(2,1)}, bf16[368,128]{1,0:T(8,128)(2,1)S(1)}, u32[]{:S(2)}) copy-start(bf16[368,128]{1,0:T(8,128)(2,1)S(1)} %corners.1.refs_6_) | copy-start | bytes 282628
  30.4 4.4 %collective-permute-start.3 = (bf16[368,128]{1,0:T(8,128)(2,1)S(1)}, bf16[368,128]{1,0:T(8,128)(2,1)S(1)}, u32[]{:S(2)}, u32[]{:S(2)}) collective-permute-start(bf16[368,128]{1,0:T(8,128)(2,1)S(1)} %corners.1.refs_6_), channel_id=1, source_target_pairs={{1,2},{3,4},{5,6},{2,1},{4,3},{6,5},{9,10},{11,12},{13,14},{10,9},... | collective-permute-start | bytes 282632 | tf_op jit(solution)/shard_map/ppermute | solution.py:584
  31.0 5.7 %collective-permute-start.2 = (bf16[368,128]{1,0:T(8,128)(2,1)S(1)}, bf16[368,128]{1,0:T(8,128)(2,1)S(1)}, u32[]{:S(2)}, u32[]{:S(2)}) collective-permute-start(bf16[368,128]{1,0:T(8,128)(2,1)S(1)} %corners.1.refs_6_), channel_id=1, source_target_pairs={{0,1},{2,3},{4,5},{6,7},{1,0},{3,2},{5,4},{7,6},{8,9},{10,11},{12,... | collective-permute-start | bytes 282632 | tf_op jit(solution)/shard_map/ppermute | solution.py:584
  34.7 2.0 %copy-start.5 = (bf16[368,128]{1,0:T(8,128)(2,1)}, bf16[368,128]{1,0:T(8,128)(2,1)S(1)}, u32[]{:S(2)}) copy-start(bf16[368,128]{1,0:T(8,128)(2,1)S(1)} %collective-permute-done.3.refs_8_) | copy-start | bytes 282628
  36.7 0.6 copy-start.6
  36.7 1.0 %copy-start.4 = (bf16[128,16,256]{2,1,0:T(8,128)(2,1)}, bf16[128,16,256]{2,1,0:T(8,128)(2,1)S(1)}, u32[]{:S(2)}) copy-start(bf16[128,16,256]{2,1,0:T(8,128)(2,1)S(1)} %all-to-all-done) | copy-start | bytes 3145732
  52.5 30.1 %all-to-all-start.1 = ((bf16[128,16,256]{2,1,0:T(8,128)(2,1)}), bf16[128,16,256]{2,1,0:T(8,128)(2,1)S(1)}, u32[]{:S(2)}, u32[]{:S(2)}) async-start(bf16[128,16,256]{2,1,0:T(8,128)(2,1)} %bitcast.26), calls=%async_computation.1 | async-start | bytes 2097152 | tf_op jit(solution)/shard_map/all_to_all | solution.py:588

commit v2 on v1

--- a/solution.py
+++ b/solution.py
@@ -534,7 +534,7 @@
         copy.wait()
 
 
-def run(kernel, outs, scratch, flops, moved, *args, name=None, far=(), limit=62914560, **rest):
+def run(kernel, outs, scratch, flops, moved, *args, name=None, far=(), limit=58 * 1024 * 1024, **rest):
     anywhere, near = pl.BlockSpec(memory_space=pl.ANY), pl.BlockSpec(memory_space=pltpu.VMEM)
     rest = rest or dict(in_specs=[anywhere if n in far else near for n in range(len(args))])
     return pl.pallas_call(

time: 84 us -> 84 us (level)
  no operation moved by 1% of the time
where the time goes in v2:
time: 84 us; the launch traced here: 83.6 us
  Pallas kernels  35.4 us (42%)
  starting transfers between devices  30.8 us (37%)
  waiting for transfers between devices  13.8 us (16%)
  local copies, waits for them, and re-layouts  2.9 us (3%)
    pallas_call x5, Pallas kernels, run(): pl.pallas_call(kernel, out_shape=[jax.ShapeDtypeStruct(shape, kind) for s...  35.4 us
    all_to_all x2, starting transfers between devices, exchange(): lax.all_to_all(blocks, ('gx', 'gy'), split_axis=0, concat_axis=0, tiled=T...  22.7 us
    all_to_all x2, waiting for transfers between devices, exchange(): lax.all_to_all(blocks, ('gx', 'gy'), split_axis=0, concat_axis=0, tiled=T...  8.13 us
    ppermute x4, starting transfers between devices, swap(): lax.ppermute(block, axis, [(i, i + 1) for i in firsts] + [(i + 1, i) for...  8.04 us
    ppermute x4, waiting for transfers between devices, swap(): lax.ppermute(block, axis, [(i, i + 1) for i in firsts] + [(i + 1, i) for...  5.64 us
    unnamed x15, local copies, waits for them, and re-layouts  2.9 us
  transfers between devices with their start and end apart: 6, of which 3 were waited for; matrix products, arithmetic and copies ran while one was open for 0% of the time, Pallas kernels for 25%

profile of v2, /device:TPU:1, one launch (start us, length us, event | category | flops | bytes accessed | tf_op | source)
XLA Modules:
  0.0 83.6 jit_solution(12048529125905212253)
XLA Ops:
  0.6 11.5 %all-to-all-start = ((bf16[128,16,256]{2,1,0:T(8,128)(2,1)}), bf16[128,16,256]{2,1,0:T(8,128)(2,1)S(1)}, u32[]{:S(2)}, u32[]{:S(2)}) async-start(bf16[128,16,256]{2,1,0:T(8,128)(2,1)} %bitcast.24), calls=%async_computation | async-start | bytes 2097152 | tf_op jit(solution)/shard_map/all_to_all | solution.py:588
  12.1 3.9 %rows.1 = (bf16[1216,128]{1,0:T(8,128)(2,1)}, bf16[1216,128]{1,0:T(8,128)(2,1)}) custom-call(f32[8192,128]{1,0:T(8,128)} %bitcast.10, f32[1024,128]{1,0:T(8,128)} %bitcast.14, f32[1024,128]{1,0:T(8,128)} %bitcast.18), custom_call_target="tpu_custom_call" | custom-call | flops 1000000 | bytes 5000000 | tf_op jit(solution)/shard_map/rows/pallas_call | solution.py:540
  16.1 1.1 %collective-permute-start = (bf16[1216,128]{1,0:T(8,128)(2,1)}, bf16[1216,128]{1,0:T(8,128)(2,1)S(1)}, u32[]{:S(2)}, u32[]{:S(2)}) collective-permute-start(bf16[1216,128]{1,0:T(8,128)(2,1)} %get-tuple-element.11), channel_id=1, source_target_pairs={{0,8},{16,24},{32,40},{48,56},{64,72},{80,88},{96,104},{112,120},{... | collective-permute-start | bytes 933896 | tf_op jit(solution)/shard_map/ppermute | solution.py:584
  17.1 2.6 %collective-permute-start.1 = (bf16[1216,128]{1,0:T(8,128)(2,1)}, bf16[1216,128]{1,0:T(8,128)(2,1)S(1)}, u32[]{:S(2)}, u32[]{:S(2)}) collective-permute-start(bf16[1216,128]{1,0:T(8,128)(2,1)} %get-tuple-element.12), channel_id=1, source_target_pairs={{8,16},{24,32},{40,48},{56,64},{72,80},{88,96},{104,112},{16,8},{3... | collective-permute-start | bytes 933896 | tf_op jit(solution)/shard_map/ppermute | solution.py:584
  19.8 5.2 %cols.1 = (bf16[320,128]{1,0:T(8,128)(2,1)}, bf16[512,256]{1,0:T(8,128)(2,1)}, bf16[512,512]{1,0:T(8,128)(2,1)}, bf16[256,512]{1,0:T(8,128)(2,1)}) custom-call(f32[8192,128]{1,0:T(8,128)} %bitcast.11, f32[1024,128]{1,0:T(8,128)} %bitcast.15, f32[1024,128]{1,0:T(8,128)} %bitcast.19, bf16[256,512]{1,0:T(8,128)(2,1)} %refs_14_.1, bf16[512,512]{1,0:T(8,128)(2,1)} %refs_13_.1, ...), custom_call_target="tpu_custom_call" | custom-call | flops 100000000 | bytes 10000000 | tf_op jit(solution)/shard_map/cols/pallas_call | solution.py:540
  25.0 0.0 collective-permute-done.from_partner.refs_4_
  25.0 0.0 copy-start
  25.0 3.7 %collective-permute-done.1.from_other.refs_5_ = bf16[1216,128]{1,0:T(8,128)(2,1)S(1)} collective-permute-done((bf16[1216,128]{1,0:T(8,128)(2,1)}, bf16[1216,128]{1,0:T(8,128)(2,1)S(1)}, u32[]{:S(2)}, u32[]{:S(2)}) %collective-permute-start.1) | collective-permute-done | bytes 311328 | tf_op jit(solution)/shard_map/ppermute | solution.py:584
  28.7 0.0 copy-start.1
  28.7 0.0 copy-start.3
  28.7 1.0 %copy-done.3 = bf16[320,128]{1,0:T(8,128)(2,1)S(1)} copy-done((bf16[320,128]{1,0:T(8,128)(2,1)S(1)}, bf16[320,128]{1,0:T(8,128)(2,1)}, u32[]{:S(2)}) %copy-start.3) | copy-done | bytes 81944
  29.6 0.7 corners.1.refs_6_
  30.3 0.0 copy-start.2
  30.4 0.7 collective-permute-start.3
  31.0 3.7 %collective-permute-start.2 = (bf16[368,128]{1,0:T(8,128)(2,1)S(1)}, bf16[368,128]{1,0:T(8,128)(2,1)S(1)}, u32[]{:S(2)}, u32[]{:S(2)}) collective-permute-start(bf16[368,128]{1,0:T(8,128)(2,1)S(1)} %corners.1.refs_6_), channel_id=1, source_target_pairs={{0,1},{2,3},{4,5},{6,7},{1,0},{3,2},{5,4},{7,6},{8,9},{10,11},{12,... | collective-permute-start | bytes 282632 | tf_op jit(solution)/shard_map/ppermute | solution.py:584
  34.7 0.0 collective-permute-done.3.refs_8_
  34.7 0.0 copy-start.5
  34.7 2.0 %collective-permute-done.2.refs_7_ = bf16[368,128]{1,0:T(8,128)(2,1)S(1)} collective-permute-done((bf16[368,128]{1,0:T(8,128)(2,1)S(1)}, bf16[368,128]{1,0:T(8,128)(2,1)S(1)}, u32[]{:S(2)}, u32[]{:S(2)}) %collective-permute-start.2) | collective-permute-done | bytes 94240 | tf_op jit(solution)/shard_map/ppermute | solution.py:584
  36.7 0.0 copy-start.6
  36.7 0.0 all-to-all-done
  36.7 0.0 copy-start.4
  36.7 0.0 copy-done
  36.7 0.0 copy-done.1
  36.7 0.0 copy-done.2
  36.7 0.0 copy-done.5
  36.7 0.6 copy-done.6
  37.3 0.4 copy-done.4
  37.7 14.8 %main.1 = (f32[64,64,128]{2,1,0:T(8,128)}, bf16[2048,256]{1,0:T(8,128)(2,1)}, bf16[1024,1024]{1,0:T(8,128)(2,1)}) custom-call(f32[64,128,128]{2,1,0:T(8,128)} %bitcast.12, f32[1024,128]{1,0:T(8,128)} %bitcast.16, f32[1024,128]{1,0:T(8,128)} %bitcast.20, f32[1008,128]{1,0:T(8,128)} %bitcast.27, bf16[1216,128]{1,0:T(8,128)(2,1)} %copy-done, ...), custom_call_target="tpu_custom_call" | custom-call | flops 4000000000 | bytes 10000000 | tf_op jit(solution)/shard_map/main/pallas_call | solution.py:540
  52.5 11.2 %all-to-all-start.1 = ((bf16[128,16,256]{2,1,0:T(8,128)(2,1)}), bf16[128,16,256]{2,1,0:T(8,128)(2,1)S(1)}, u32[]{:S(2)}, u32[]{:S(2)}) async-start(bf16[128,16,256]{2,1,0:T(8,128)(2,1)} %bitcast.26), calls=%async_computation.1 | async-start | bytes 2097152 | tf_op jit(solution)/shard_map/all_to_all | solution.py:588
  63.7 10.8 %last_fields.1 = f32[64,128,128]{2,1,0:T(8,128)} custom-call(f32[64,128,128]{2,1,0:T(8,128)} %bitcast.13, f32[1024,128]{1,0:T(8,128)} %bitcast.17, f32[1024,128]{1,0:T(8,128)} %bitcast.21, f32[1008,128]{1,0:T(8,128)} %bitcast.28, bf16[1216,128]{1,0:T(8,128)(2,1)} %copy-done, bf16[1216,128]{1,0:T(8,128)(2,1)} %copy-done.1, bf16[368,128]{1,0:T(8,128)(2,1)} %copy-done.2, ...), custom_call_target="tpu_custom_call" | custom-call | flops 1000000000 | bytes 20000000 | tf_op jit(solution)/shard_map/last_fields/pallas_call | solution.py:540
  74.5 8.1 %all-to-all-done.1 = bf16[128,16,256]{2,1,0:T(8,128)(2,1)S(1)} async-done(((bf16[128,16,256]{2,1,0:T(8,128)(2,1)}), bf16[128,16,256]{2,1,0:T(8,128)(2,1)S(1)}, u32[]{:S(2)}, u32[]{:S(2)}) %all-to-all-start.1) | async-done | bytes 1048608 | tf_op jit(solution)/shard_map/all_to_all | solution.py:588
  82.6 1.0 %copy.11 = bf16[2048,256]{1,0:T(8,128)(2,1)} copy(bf16[2048,256]{1,0:T(8,128)(2,1)S(1)} %bitcast.22) | data formatting | bytes 2097152
Async XLA Ops:
  0.6 36.1 %all-to-all-start = ((bf16[128,16,256]{2,1,0:T(8,128)(2,1)}), bf16[128,16,256]{2,1,0:T(8,128)(2,1)S(1)}, u32[]{:S(2)}, u32[]{:S(2)}) async-start(bf16[128,16,256]{2,1,0:T(8,128)(2,1)} %bitcast.24), calls=%async_computation | async-start | bytes 2097152 | tf_op jit(solution)/shard_map/all_to_all | solution.py:588
  16.1 8.9 %collective-permute-start = (bf16[1216,128]{1,0:T(8,128)(2,1)}, bf16[1216,128]{1,0:T(8,128)(2,1)S(1)}, u32[]{:S(2)}, u32[]{:S(2)}) collective-permute-start(bf16[1216,128]{1,0:T(8,128)(2,1)} %get-tuple-element.11), channel_id=1, source_target_pairs={{0,8},{16,24},{32,40},{48,56},{64,72},{80,88},{96,104},{112,120},{... | collective-permute-start | bytes 933896 | tf_op jit(solution)/shard_map/ppermute | solution.py:584
  17.1 11.5 %collective-permute-start.1 = (bf16[1216,128]{1,0:T(8,128)(2,1)}, bf16[1216,128]{1,0:T(8,128)(2,1)S(1)}, u32[]{:S(2)}, u32[]{:S(2)}) collective-permute-start(bf16[1216,128]{1,0:T(8,128)(2,1)} %get-tuple-element.12), channel_id=1, source_target_pairs={{8,16},{24,32},{40,48},{56,64},{72,80},{88,96},{104,112},{16,8},{3... | collective-permute-start | bytes 933896 | tf_op jit(solution)/shard_map/ppermute | solution.py:584
  25.0 11.7 %copy-start = (bf16[1216,128]{1,0:T(8,128)(2,1)}, bf16[1216,128]{1,0:T(8,128)(2,1)S(1)}, u32[]{:S(2)}) copy-start(bf16[1216,128]{1,0:T(8,128)(2,1)S(1)} %collective-permute-done.from_partner.refs_4_) | copy-start | bytes 933892
  28.7 8.0 %copy-start.1 = (bf16[1216,128]{1,0:T(8,128)(2,1)}, bf16[1216,128]{1,0:T(8,128)(2,1)S(1)}, u32[]{:S(2)}) copy-start(bf16[1216,128]{1,0:T(8,128)(2,1)S(1)} %collective-permute-done.1.from_other.refs_5_) | copy-start | bytes 933892
  28.7 1.0 %copy-start.3 = (bf16[320,128]{1,0:T(8,128)(2,1)S(1)}, bf16[320,128]{1,0:T(8,128)(2,1)}, u32[]{:S(2)}) copy-start(bf16[320,128]{1,0:T(8,128)(2,1)} %get-tuple-element.13.edges) | copy-start | bytes 245764
  30.3 6.4 %copy-start.2 = (bf16[368,128]{1,0:T(8,128)(2,1)}, bf16[368,128]{1,0:T(8,128)(2,1)S(1)}, u32[]{:S(2)}) copy-start(bf16[368,128]{1,0:T(8,128)(2,1)S(1)} %corners.1.refs_6_) | copy-start | bytes 282628
  30.4 4.4 %collective-permute-start.3 = (bf16[368,128]{1,0:T(8,128)(2,1)S(1)}, bf16[368,128]{1,0:T(8,128)(2,1)S(1)}, u32[]{:S(2)}, u32[]{:S(2)}) collective-permute-start(bf16[368,128]{1,0:T(8,128)(2,1)S(1)} %corners.1.refs_6_), channel_id=1, source_target_pairs={{1,2},{3,4},{5,6},{2,1},{4,3},{6,5},{9,10},{11,12},{13,14},{10,9},... | collective-permute-start | bytes 282632 | tf_op jit(solution)/shard_map/ppermute | solution.py:584
  31.0 5.7 %collective-permute-start.2 = (bf16[368,128]{1,0:T(8,128)(2,1)S(1)}, bf16[368,128]{1,0:T(8,128)(2,1)S(1)}, u32[]{:S(2)}, u32[]{:S(2)}) collective-permute-start(bf16[368,128]{1,0:T(8,128)(2,1)S(1)} %corners.1.refs_6_), channel_id=1, source_target_pairs={{0,1},{2,3},{4,5},{6,7},{1,0},{3,2},{5,4},{7,6},{8,9},{10,11},{12,... | collective-permute-start | bytes 282632 | tf_op jit(solution)/shard_map/ppermute | solution.py:584
  34.7 2.0 %copy-start.5 = (bf16[368,128]{1,0:T(8,128)(2,1)}, bf16[368,128]{1,0:T(8,128)(2,1)S(1)}, u32[]{:S(2)}) copy-start(bf16[368,128]{1,0:T(8,128)(2,1)S(1)} %collective-permute-done.3.refs_8_) | copy-start | bytes 282628
  36.7 0.6 copy-start.6
  36.7 1.0 %copy-start.4 = (bf16[128,16,256]{2,1,0:T(8,128)(2,1)}, bf16[128,16,256]{2,1,0:T(8,128)(2,1)S(1)}, u32[]{:S(2)}) copy-start(bf16[128,16,256]{2,1,0:T(8,128)(2,1)S(1)} %all-to-all-done) | copy-start | bytes 3145732
  52.5 30.1 %all-to-all-start.1 = ((bf16[128,16,256]{2,1,0:T(8,128)(2,1)}), bf16[128,16,256]{2,1,0:T(8,128)(2,1)S(1)}, u32[]{:S(2)}, u32[]{:S(2)}) async-start(bf16[128,16,256]{2,1,0:T(8,128)(2,1)} %bitcast.26), calls=%async_computation.1 | async-start | bytes 2097152 | tf_op jit(solution)/shard_map/all_to_all | solution.py:588
